TPU v7x, 32 devices: a whole 2x2x4 slice. The times are simulated.
32 devices in a mesh: rollout: 4 (over y, x), section: 4 (over z), tensor: 2 (over core).
Axes of the slice: x: 2, y: 2, z: 4, core: 2. Of those that a mesh axis runs over, the one named last changes fastest.
Arguments:
- entering: bfloat16 [4, 128, 8192], P('section', 'tensor', 'rollout')
- arriving: bfloat16 [2, 128, 8192], P(None, 'tensor', 'rollout')
- w_query: bfloat16 [4, 8192, 4096], P('section', 'rollout', 'tensor'), may hold values from -0.0625 to 0.0625
- w_keyval: bfloat16 [4, 8192, 2, 1024], P('section', 'rollout', None, 'tensor'), may hold values from -0.0625 to 0.0625
- w_out: bfloat16 [4, 4096, 8192], P('section', 'tensor', 'rollout'), may hold values from -0.75 to 0.75
- query_bias: bfloat16 [4, 4096], P('section', 'tensor')
- keyval_bias: bfloat16 [4, 2, 1024], P('section', None, 'tensor'), may hold values from -3 to 3
- norm_gain: bfloat16 [4, 8192], P('section', 'rollout'), may hold values from 0.5 to 1.5
- resident_kv: bfloat16 [4, 4, 1120, 2, 1024], P('rollout', 'section', None, None, 'tensor')
- resumed_pages: int32 [4], replicated, may hold values from 24 to 32, as said below
- section_active: int32 [4], replicated, may hold values from 0 to 1, as said below
- block_table: int32 [4, 4, 38, 2], replicated, may hold values from 0 to 37, as said below
Outputs:
- section_out: bfloat16 [4, 3, 128, 8192], P('section', None, 'tensor', 'rollout')
- page_pool: bfloat16 [4, 4, 38, 32, 2, 1024], P('rollout', 'section', None, None, None, 'tensor')
Inputs may be any that keep to these rules, and one draw needn't show every extreme that they name: `resumed_pages`: some rollout has exactly 32 pages. `section_active`: exactly 3 sections hold a layer. `block_table`: entry [..., 0] names a decode device (rollout index times 4 plus section index) and entry [..., 1] a slot there; every pair of device and slot is named by exactly one page; the 38 pages of each rollout and section name any one decode device at most 3 times, and each of them reaches that bound for some device.
All inputs are finite; a program needn't handle non-finite values.
Results may differ from a plain program's by a relative error of at most 0.029.
Values may be sent and summed in bfloat16 or wider, within the bound.
A program may use at most 128 MiB of HBM per device.

v0:
```python
import functools
import math

import jax
import jax.numpy as jnp
import numpy as np
from jax import lax
from jax.experimental import pallas as pl
from jax.experimental.pallas import tpu as pltpu
from jax.sharding import PartitionSpec as P

HD = 128
BLOCK = 32
BLOCKS = 3
PAGE = 32
CHUNK = 512
EPS = 1e-06
MESH = pl.DeviceIdType.MESH


def remote(src, dst, send, recv, **where):
    return pltpu.make_async_remote_copy(
        src_ref=src, dst_ref=dst, send_sem=send, recv_sem=recv, device_id=where, device_id_type=MESH
    )


def steps_kernel(
    dims,
    resumed,
    layer_on,
    pack_pages,
    entering,
    arriving,
    gain,
    query_bias,
    keyval_bias,
    freq,
    w_query,
    w_key,
    w_val,
    w_out,
    resident_keys,
    resident_vals,
    out,
    landed,
    fresh,
    wcat,
    wout,
    kv,
    packed,
    own_x,
    peer_x,
    normed,
    part,
    squares,
    part_in,
    squares_in,
    heads,
    attended,
    mixed,
    mixed_in,
    load_sem,
    fwd_s,
    fwd_r,
    sq_s,
    sq_r,
    rs_s,
    rs_r,
    ag_s,
    ag_r,
    ex_s,
    ex_r,
    hand_s,
    hand_r,
    ship_s,
    ship_r,
    fz_s,
    fz_r,
    fx_s,
    fx_r,
    own_sem,
):
    R, S, context = dims
    r = lax.axis_index("rollout")
    s = lax.axis_index("section")
    t = lax.axis_index("tensor")
    other = 1 - t
    token_rows, width = entering.shape
    qw = w_query.shape[1]
    kw = resident_keys.shape[2]
    held = resident_keys.shape[0]
    dests = R * S
    me = r * S + s
    n_rs = wcat.shape[1] // CHUNK
    n_out = wout.shape[1] // CHUNK
    n_kv = kw // HD
    group = qw // kw
    group_width = group * HD
    half = token_rows
    length = (resumed[r] + (S - 1 - s)) * PAGE

    loads = [
        pltpu.make_async_copy(resident_keys, kv.at[pl.ds(0, held), :, pl.ds(0, kw)], load_sem.at[0]),
        pltpu.make_async_copy(resident_vals, kv.at[pl.ds(0, held), :, pl.ds(kw, kw)], load_sem.at[1]),
        pltpu.make_async_copy(w_query, wcat.at[:, pl.ds(0, qw)], load_sem.at[2]),
        pltpu.make_async_copy(w_key, wcat.at[:, pl.ds(qw, kw)], load_sem.at[3]),
        pltpu.make_async_copy(w_val, wcat.at[:, pl.ds(qw + kw, kw)], load_sem.at[4]),
        pltpu.make_async_copy(w_out, wout, load_sem.at[5]),
    ]
    for load in loads:
        load.start()

    barrier = pltpu.get_barrier_semaphore()

    def greet(o, carry):
        d = lax.rem(me + o, dests)
        pl.semaphore_signal(
            barrier, inc=1, device_id={"rollout": d // S, "section": lax.rem(d, S)}, device_id_type=MESH
        )
        return carry

    lax.fori_loop(1, dests, greet, 0)
    pl.semaphore_signal(barrier, inc=1, device_id={"tensor": other}, device_id_type=MESH)

    own_x[0] = entering[...]

    @pl.when(s == 0)
    def _():
        for k in range(1, BLOCKS):
            own_x[k] = arriving[k - 1]

    spare = kv.shape[0] - held
    kv[pl.ds(held, spare)] = jnp.zeros((spare, PAGE, 2 * kw), jnp.bfloat16)
    pl.semaphore_wait(barrier, dests)

    def cols(c, size=CHUNK):
        return pl.ds(pl.multiple_of(c * size, size), size)

    def rows_of(b):
        return pl.ds(pl.multiple_of(b * BLOCK, BLOCK), BLOCK)

    def fwd(k, c):
        return remote(own_x.at[k, :, cols(c)], peer_x.at[:, cols(c)], fwd_s.at[c], fwd_r.at[c], tensor=other)

    def hand(k, c):
        return remote(
            out.at[k, :, cols(c)],
            own_x.at[k + 1, :, cols(c)],
            hand_s.at[k, c],
            hand_r.at[k, c],
            section=jnp.minimum(s + 1, S - 1),
        )

    def ahead(j):
        return lax.rem(r + j, R)

    def behind(j):
        return lax.rem(r + R - j, R)

    def sq(j):
        return remote(
            squares.at[rows_of(ahead(j))], squares_in.at[rows_of(r)], sq_s.at[j], sq_r.at[j], rollout=ahead(j)
        )

    def rs(c, j):
        return remote(
            part.at[rows_of(ahead(j)), cols(c)],
            part_in.at[rows_of(r), cols(c)],
            rs_s.at[c, j],
            rs_r.at[c, j],
            rollout=ahead(j),
        )

    def ag(c, j):
        ref = attended.at[rows_of(r), cols(c, group_width)]
        return remote(ref, ref, ag_s.at[c, j], ag_r.at[c, j], rollout=ahead(j))

    def ex(c):
        return remote(
            mixed.at[pl.ds(pl.multiple_of(other * half, BLOCK), half), cols(c)],
            mixed_in.at[:, cols(c)],
            ex_s.at[c],
            ex_r.at[c],
            tensor=other,
        )

    def ship(o):
        to_r = lax.rem(r + o // S, R)
        to_s = lax.rem(s + lax.rem(o, S), S)
        return remote(
            packed.at[to_r * S + to_s], landed.at[me], ship_s.at[o], ship_r.at[o], rollout=to_r, section=to_s
        )

    def ship_mixed(low, high):
        def one(m, carry):
            ship((m // (S - 1) + 1) * S + lax.rem(m, S - 1) + 1).start()
            return carry

        lax.fori_loop(low, high, one, 0)

    def fz(k, j):
        return remote(
            kv.at[held + k], fresh.at[k, r, s], fz_s.at[k, j], fz_r.at[k, j], section=lax.rem(s + j, S)
        )

    def fx(k, j):
        return remote(fresh.at[k, r], fresh.at[k, r], fx_s.at[k, j], fx_r.at[k, j], rollout=ahead(j))

    def own_page(k):
        return pltpu.make_async_copy(kv.at[held + k], fresh.at[k, r, s], own_sem.at[k])

    own_slots = pltpu.make_async_copy(packed.at[me], landed.at[me], own_sem.at[BLOCKS])

    def spread(k):
        own_page(k).wait()
        for j in range(1, S):
            fz(k, j).wait()
        for j in range(1, R):
            fx(k, j).start()

    mixed_count = (R - 1) * (S - 1)
    loads[0].wait()
    loads[1].wait()

    def pack(d, carry):
        for c in range(packed.shape[1]):
            packed[d, c] = kv[pack_pages[d * packed.shape[1] + c]]
        return carry

    lax.fori_loop(0, dests, pack, 0)
    own_slots.start()
    for o in range(1, S):
        ship(jnp.int32(o)).start()

    def ship_plane(o, carry):
        ship(o * S).start()
        return carry

    lax.fori_loop(1, R, ship_plane, 0)

    def step_body(k, carry):
        for c in range(n_out):
            @pl.when((k > 0) & (s > 0))
            def _(c=c):
                hand(k - 1, c).wait_recv()

            fwd(k, c).start()

        def norm(ref, base):
            def body(i, carry):
                xf = ref[rows_of(i), :].astype(jnp.float32)
                ms = jnp.sum(xf * xf, axis=1, keepdims=True) / width
                rows = pl.ds(pl.multiple_of(base + i * BLOCK, BLOCK), BLOCK)
                normed[rows, :] = (xf * lax.rsqrt(ms + EPS) * gain[...].astype(jnp.float32)).astype(
                    jnp.bfloat16
                )
                squares[rows, :] = jnp.broadcast_to(ms, (BLOCK, HD))
                return carry

            lax.fori_loop(0, half // BLOCK, body, 0)

        norm(own_x.at[k], t * half)
        for c in range(n_out):
            fwd(k, c).wait()
        norm(peer_x, other * half)
        for j in range(1, R):
            sq(j).start()

        @pl.when(k == 0)
        def _():
            for load in loads[2:5]:
                load.wait()

        def project(c, carry):
            part[:, cols(c)] = jnp.dot(
                normed[...], wcat[:, cols(c)], preferred_element_type=jnp.float32
            ).astype(jnp.bfloat16)
            for j in range(1, R):
                rs(c, j).start()
            return carry

        lax.fori_loop(0, n_rs, project, 0)

        @pl.when(k > 0)
        def _():
            spread(k - 1)

        for j in range(1, R):
            sq(j).wait()
        ms = [squares[rows_of(r), :]] + [squares_in[rows_of(behind(j)), :] for j in range(1, R)]
        whole = lax.rsqrt(sum(ms) / R + EPS)
        ratios = []
        for m in ms:
            local = lax.rsqrt(m + EPS)
            ratios.append(jnp.where(local > 0, whole / jnp.where(local > 0, local, 1.0), 0.0)[:, :1])
        angle = (length + k * BLOCK + lax.broadcasted_iota(jnp.int32, (BLOCK, HD), 0)).astype(
            jnp.float32
        ) * freq[...]
        lane = lax.broadcasted_iota(jnp.int32, (BLOCK, HD), 1)
        cos = jnp.cos(angle)
        sin = jnp.sin(angle)
        sin = jnp.where(lane < HD // 2, -sin, sin)

        def rotate(v):
            return v * cos + pltpu.roll(v, HD // 2, 1) * sin

        shifts = keyval_bias[...].astype(jnp.float32)
        for c in range(n_rs):
            for j in range(1, R):
                rs(c, j).wait()
            acc = part[rows_of(r), cols(c)].astype(jnp.float32) * ratios[0]
            for j in range(1, R):
                acc = acc + part_in[rows_of(behind(j)), cols(c)].astype(jnp.float32) * ratios[j]
            low = c * CHUNK
            for h in range(CHUNK // HD):
                at = low + h * HD
                one = acc[:, h * HD : (h + 1) * HD]
                if at < qw:
                    one = rotate(one + query_bias[:, at : at + HD].astype(jnp.float32))
                    heads[at // HD * BLOCK : (at // HD + 1) * BLOCK, :] = one.astype(jnp.bfloat16)
                else:
                    at = at - qw
                    one = one + shifts[at // kw : at // kw + 1, at % kw : at % kw + HD]
                    if at < kw:
                        one = rotate(one)
                    kv[held + k, :, at : at + HD] = one.astype(jnp.bfloat16)
        own_page(k).start()
        for j in range(1, S):
            fz(k, j).start()

        total = kv.shape[0] * PAGE
        column = lax.broadcasted_iota(jnp.int32, (group * BLOCK, total), 1)
        token = lax.rem(lax.broadcasted_iota(jnp.int32, (group * BLOCK, total), 0), BLOCK)
        seen = (column < length) | ((column >= context) & (column - context <= k * BLOCK + token))
        for g in range(n_kv):
            at = g * HD
            scores = lax.dot_general(
                heads[g * group * BLOCK : (g + 1) * group * BLOCK, :],
                kv[:, :, at : at + HD].reshape(total, HD),
                (((1,), (1,)), ((), ())),
                preferred_element_type=jnp.float32,
            )
            scores = jnp.where(seen, scores * (1.0 / math.sqrt(HD)), -1e30)
            powers = jnp.exp(scores - jnp.max(scores, axis=-1, keepdims=True))
            total_power = jnp.sum(powers, axis=-1, keepdims=True)
            got = jnp.dot(
                powers.astype(jnp.bfloat16),
                kv[:, :, kw + at : kw + at + HD].reshape(total, HD),
                preferred_element_type=jnp.float32,
            )
            got = (got / total_power).astype(jnp.bfloat16)
            for i in range(group):
                lane = (g * group + i) * HD
                attended[rows_of(r), lane : lane + HD] = got[i * BLOCK : (i + 1) * BLOCK, :]
            for j in range(1, R):
                ag(g, j).start()

        @pl.when(k == 0)
        def _():
            loads[5].wait()

        @pl.when(k == BLOCKS - 1)
        def _():
            ship_mixed(mixed_count * 7 // 9, mixed_count)
            spread(BLOCKS - 1)

        for g in range(n_kv):
            for j in range(1, R):
                ag(g, j).wait()

        @pl.when(k == 0)
        def _():
            ship_mixed(0, mixed_count * 4 // 9)

        @pl.when(k == 1)
        def _():
            ship_mixed(mixed_count * 4 // 9, mixed_count * 7 // 9)

        def project_out(c, carry):
            mixed[:, cols(c)] = jnp.dot(
                attended[...], wout[:, cols(c)], preferred_element_type=jnp.float32
            ).astype(jnp.bfloat16)
            ex(c).start()
            return carry

        lax.fori_loop(0, n_out, project_out, 0)
        active = layer_on[s].astype(jnp.float32)

        def finish(c, carry):
            ex(c).wait()
            own = mixed[pl.ds(pl.multiple_of(t * half, BLOCK), half), cols(c)].astype(jnp.float32)
            summed = own + mixed_in[:, cols(c)].astype(jnp.float32)
            base = own_x[k, :, cols(c)].astype(jnp.float32)
            out[k, :, cols(c)] = (base + active * summed).astype(jnp.bfloat16)

            @pl.when((k < BLOCKS - 1) & (s < S - 1))
            def _():
                hand(k, c).start()

            return carry

        lax.fori_loop(0, n_out, finish, 0)
        return carry

    lax.fori_loop(0, BLOCKS, step_body, 0)

    @pl.when(s < S - 1)
    def _():
        for k in range(BLOCKS - 1):
            for c in range(n_out):
                hand(k, c).wait_send()

    def ship_wait(o, carry):
        ship(o).wait()
        return carry

    lax.fori_loop(1, dests, ship_wait, 0)
    own_slots.wait()
    for k in range(BLOCKS):
        for j in range(1, R):
            fx(k, j).wait()


def place_kernel(slots, kind, place, landed, fresh, pool):
    def body(i, carry):
        @pl.when(kind[i] == 0)
        def _():
            pool[i] = jnp.zeros_like(pool[i])

        @pl.when(kind[i] == 1)
        def _():
            pool[i] = landed[place[i]]

        @pl.when(kind[i] == 2)
        def _():
            pool[i] = fresh[place[i]]

        return carry

    lax.fori_loop(0, slots, body, 0)


def local(
    entering,
    arriving,
    w_query,
    w_keyval,
    w_out,
    query_bias,
    keyval_bias,
    norm_gain,
    resident_kv,
    resumed_pages,
    section_active,
    block_table,
):
    R = lax.axis_size("rollout")
    S = lax.axis_size("section")
    r = lax.axis_index("rollout")
    s = lax.axis_index("section")
    width_block, qw = w_query.shape[1:]
    kw = w_keyval.shape[3]
    token_rows = entering.shape[1]
    rows = R * BLOCK
    out_width = w_out.shape[2]
    context = resident_kv.shape[2]
    page_count = block_table.shape[2]
    dests = R * S
    cap = (page_count + dests - 1) // dests
    me = r * S + s

    routing = block_table.reshape(dests, page_count, 2)
    targets = routing[:, :, 0]
    slot_ids = routing[:, :, 1]
    page_ids = jnp.arange(page_count, dtype=jnp.int32)
    before = page_ids[None, :] < page_ids[:, None]
    ranks = jnp.sum(
        ((targets[:, :, None] == targets[:, None, :]) & before[None]).astype(jnp.int32), axis=2
    )
    column = targets[me] * cap + ranks[me]
    buffer_ids = jnp.arange(dests * cap, dtype=jnp.int32)
    source_pages = jnp.minimum(page_ids, context // PAGE - 1)
    pack_pages = jnp.sum(
        jnp.where(buffer_ids[:, None] == column[None, :], source_pages[None, :], 0), axis=1
    ).astype(jnp.int32)
    sources = jnp.arange(dests, dtype=jnp.int32)
    first_of = (resumed_pages[:, None] + (S - 1 - jnp.arange(S, dtype=jnp.int32))[None, :]).reshape(-1)
    switched_on = jnp.broadcast_to(section_active[None, :], (R, S)).reshape(-1) > 0
    turn = page_ids[None, :] - first_of[:, None]
    alive = (turn < BLOCKS) & switched_on[:, None]
    kinds = jnp.where(alive, jnp.where(turn >= 0, 2, 1), 0)
    places = jnp.where(
        kinds == 2,
        jnp.clip(turn, 0, BLOCKS - 1) * dests + sources[:, None],
        sources[:, None] * cap + jnp.minimum(ranks, cap - 1),
    )
    codes = (kinds * (BLOCKS * dests + dests * cap) + places).reshape(-1)
    hit = (targets == me).reshape(-1)[None, :] & (slot_ids.reshape(-1)[None, :] == page_ids[:, None])
    code = jnp.sum(jnp.where(hit, codes[None, :], 0), axis=1).astype(jnp.int32)
    base = BLOCKS * dests + dests * cap
    kind, place = code // base, code % base

    freq = np.power(1000000.0, -np.arange(HD // 2) * (2.0 / HD)).astype(np.float32)
    freq = jnp.asarray(np.concatenate([freq, freq])[None, :])

    resident = resident_kv[0, 0].reshape(context // PAGE, PAGE, 2, kw)
    page_shape = (PAGE, 2 * kw)
    bf16 = jnp.bfloat16
    f32 = jnp.float32
    anywhere = pl.BlockSpec(memory_space=pl.ANY)
    vmem = pl.BlockSpec(memory_space=pltpu.VMEM)
    smem = pl.BlockSpec(memory_space=pltpu.SMEM)
    dma = pltpu.SemaphoreType.DMA

    total = -(-(context + BLOCKS * BLOCK) // HD) * HD
    n_rs = (qw + 2 * kw) // CHUNK
    n_out = out_width // CHUNK
    n_kv = kw // HD
    section_out, landed, fresh = pl.pallas_call(
        functools.partial(steps_kernel, (R, S, context)),
        out_shape=(
            jax.ShapeDtypeStruct((BLOCKS, token_rows, out_width), bf16),
            jax.ShapeDtypeStruct((dests, cap) + page_shape, bf16),
            jax.ShapeDtypeStruct((BLOCKS, R, S) + page_shape, bf16),
        ),
        in_specs=[smem] * 3 + [vmem] * 6 + [anywhere] * 6,
        out_specs=(vmem, anywhere, vmem if dests <= 16 else anywhere),
        scratch_shapes=[
            pltpu.VMEM((width_block, qw + 2 * kw), bf16),
            pltpu.VMEM((qw, out_width), bf16),
            pltpu.VMEM((total // PAGE,) + page_shape, bf16),
            pltpu.VMEM((dests, cap) + page_shape, bf16),
            pltpu.VMEM((BLOCKS, token_rows, width_block), bf16),
            pltpu.VMEM((token_rows, width_block), bf16),
            pltpu.VMEM((rows, width_block), bf16),
            pltpu.VMEM((rows, qw + 2 * kw), bf16),
            pltpu.VMEM((rows, HD), f32),
            pltpu.VMEM((rows, qw + 2 * kw), bf16),
            pltpu.VMEM((rows, HD), f32),
            pltpu.VMEM((qw // HD * BLOCK, HD), bf16),
            pltpu.VMEM((rows, qw), bf16),
            pltpu.VMEM((rows, out_width), bf16),
            pltpu.VMEM((token_rows, out_width), bf16),
            dma((6,)),
            dma((n_out,)),
            dma((n_out,)),
            dma((R,)),
            dma((R,)),
            dma((n_rs, R)),
            dma((n_rs, R)),
            dma((n_kv, R)),
            dma((n_kv, R)),
            dma((n_out,)),
            dma((n_out,)),
            dma((BLOCKS, n_out)),
            dma((BLOCKS, n_out)),
            dma((dests,)),
            dma((dests,)),
            dma((BLOCKS, S)),
            dma((BLOCKS, S)),
            dma((BLOCKS, R)),
            dma((BLOCKS, R)),
            dma((BLOCKS + 1,)),
        ],
        compiler_params=pltpu.CompilerParams(
            collective_id=0, has_side_effects=True, vmem_limit_bytes=60 * 1024 * 1024
        ),
        name="relay_steps",
    )(
        resumed_pages,
        section_active,
        pack_pages,
        entering[0],
        arriving,
        norm_gain,
        query_bias,
        keyval_bias[0],
        freq,
        w_query[0],
        w_keyval[0, :, 0],
        w_keyval[0, :, 1],
        w_out[0],
        resident[:, :, 0],
        resident[:, :, 1],
    )

    pool = pl.pallas_call(
        functools.partial(place_kernel, page_count),
        out_shape=jax.ShapeDtypeStruct((page_count,) + page_shape, bf16),
        in_specs=[smem, smem, vmem, vmem],
        out_specs=vmem,
        compiler_params=pltpu.CompilerParams(vmem_limit_bytes=48 * 1024 * 1024),
        name="place_pages",
    )(
        kind,
        place,
        landed.reshape((dests * cap,) + page_shape),
        fresh.reshape((BLOCKS * dests,) + page_shape),
    )
    return (section_out[None], pool.reshape(1, 1, page_count, PAGE, 2, kw))


def solution(mesh):
    in_specs = (
        P("section", "tensor", "rollout"),
        P(None, "tensor", "rollout"),
        P("section", "rollout", "tensor"),
        P("section", "rollout", None, "tensor"),
        P("section", "tensor", "rollout"),
        P("section", "tensor"),
        P("section", None, "tensor"),
        P("section", "rollout"),
        P("rollout", "section", None, None, "tensor"),
        P(),
        P(),
        P(),
    )
    out_specs = (
        P("section", None, "tensor", "rollout"),
        P("rollout", "section", None, None, None, "tensor"),
    )
    return jax.shard_map(local, mesh=mesh, in_specs=in_specs, out_specs=out_specs, check_vma=False)
```

profile of v0, /device:TPU:8, one launch (start us, length us, event | category | flops | bytes accessed | tf_op | source)
XLA Modules:
  0.0 194.1 jit_solution(9255567341069592258)
XLA Ops:
  0.6 0.8 slice_reduce_fusion
  1.5 0.1 copy.30
  1.6 0.1 copy.29
  1.7 0.8 convert_reduce_fusion
  2.5 0.2 add_reduce_fusion
  2.7 0.6 select_reduce_fusion.1.pack_pages
  3.3 8.9 %fusion.4 = (bf16[1,2048,1,512]{3,2,1,0:T(2,128)(2,1)S(1)}, bf16[1,2048,1,512]{3,2,1,0:T(2,128)(2,1)S(1)}) fusion(bf16[1,2048,2,512]{3,2,1,0:T(2,128)(2,1)} %param.16), kind=kLoop, calls=%fused_computation.28 | loop fusion | bytes 8388608 | tf_op jit(solution)/shard_map/slice | solution.py:581
  12.3 0.0 copy-start.1
  12.3 3.3 %copy_bitcast_fusion = (bf16[2048,512]{1,0:T(8,128)(2,1)}, bf16[2048,512]{1,0:T(8,128)(2,1)}) fusion(bf16[1,2048,1,512]{3,2,1,0:T(2,128)(2,1)S(1)} %get-tuple-element.8, bf16[1,2048,1,512]{3,2,1,0:T(2,128)(2,1)S(1)} %get-tuple-element.9), kind=kLoop, calls=%fused_computation | loop fusion | bytes 8388608 | tf_op jit(solution)/shard_map/squeeze | solution.py:581
  15.6 0.0 copy-done.1
  15.6 0.4 copy.33
  15.9 1.6 slice_bitcast_fusion
  17.6 0.0 copy-start.3
  17.6 0.0 copy-start.4
  17.6 166.7 %relay_steps.1 = (bf16[3,64,2048]{2,1,0:T(8,128)(2,1)}, bf16[16,3,32,1024]{3,2,1,0:T(8,128)(2,1)}, bf16[3,4,4,32,1024]{4,3,2,1,0:T(8,128)(2,1)}) custom-call(s32[4]{0:T(128)} %resumed.1, s32[4]{0:T(128)} %layer_on.1, s32[48]{0:T(128)} %select_reduce_fusion.1.pack_pages, bf16[64,2048]{1,0:T(8,128)(2,1)} %bitcast.30, bf16[2,64,2048]{2,1,0:T(8,128)(2,1)} %arriving.1, ...), custom_call_target="tpu_custom_call" | custom-call | tf_op jit(solution)/shard_map/relay_steps/pallas_call | solution.py:519
  184.3 0.1 eq.77
  184.4 0.0 copy-done.3
  184.4 0.1 broadcast_add_fusion
  184.5 0.1 add.81
  184.5 0.0 copy-done.4
  184.6 0.1 gt.12
  184.7 0.1 copy.34
  184.8 0.1 reshape.166
  184.8 0.1 eq.78
  184.9 0.1 select_reduce_fusion
  185.1 0.0 copy-start
  185.1 1.9 copy-done
  187.0 3.2 %place_pages.1 = bf16[38,32,1024]{2,1,0:T(8,128)(2,1)S(1)} custom-call(s32[38]{0:T(128)S(1)} %get-tuple-element.15.kind, s32[38]{0:T(128)S(1)} %get-tuple-element.14.place, bf16[48,32,1024]{2,1,0:T(8,128)(2,1)S(1)} %bitcast.24, bf16[48,32,1024]{2,1,0:T(8,128)(2,1)} %bitcast.28), custom_call_target="tpu_custom_call" | custom-call | tf_op jit(solution)/shard_map/place_pages/pallas_call | solution.py:587
  190.2 0.0 copy-start.2
  190.2 3.0 %reshape.160 = bf16[1,1,38,32,2,512]{5,4,3,2,1,0:T(2,128)(2,1)} reshape(bf16[38,32,1024]{2,1,0:T(8,128)(2,1)S(1)} %place_pages.1) | data formatting | bytes 4980736 | tf_op jit(solution)/shard_map/reshape | solution.py:600
  193.2 0.0 copy-done.2
  193.2 0.9 copy.41
  (10 shorter events, 0.1 us)
Async XLA Ops:
  12.3 3.3 %copy-start.1 = (bf16[1,1,1120,2,512]{4,3,2,1,0:T(2,128)(2,1)S(1)}, bf16[1,1,1120,2,512]{4,3,2,1,0:T(2,128)(2,1)}, u32[]{:S(2)}) copy-start(bf16[1,1,1120,2,512]{4,3,2,1,0:T(2,128)(2,1)} %param.21) | copy-start | bytes 6881284
  17.6 166.8 %copy-start.3 = (s32[4]{0:T(128)S(1)}, s32[4]{0:T(128)}, u32[]{:S(2)}) copy-start(s32[4]{0:T(128)} %resumed.1) | copy-start | bytes 52
  17.6 167.0 %copy-start.4 = (s32[4]{0:T(128)S(1)}, s32[4]{0:T(128)}, u32[]{:S(2)}) copy-start(s32[4]{0:T(128)} %layer_on.1) | copy-start | bytes 52
  185.1 1.9 copy-start
  190.2 3.1 %copy-start.2 = (bf16[3,64,2048]{2,1,0:T(8,128)(2,1)S(1)}, bf16[3,64,2048]{2,1,0:T(8,128)(2,1)}, u32[]{:S(2)}) copy-start(bf16[3,64,2048]{2,1,0:T(8,128)(2,1)} %get-tuple-element.5) | copy-start | bytes 2359300
where the time goes:
time: 197 us; the launch traced here: 194 us
  Pallas kernels  170 us (86%)
  local copies, waits for them, and re-layouts  21.6 us (11%)
    pallas_call x1, Pallas kernels, local(): pl.pallas_call(functools.partial(steps_kernel, (R, S, context)), out_shap...  167 us
    slice x1, local copies, waits for them, and re-layouts, local(): w_keyval[0, :, 1]  8.94 us

commit v1 on v0

--- a/solution.py
+++ b/solution.py
@@ -36,8 +36,7 @@
     keyval_bias,
     freq,
     w_query,
-    w_key,
-    w_val,
+    w_keyval,
     w_out,
     resident_keys,
     resident_vals,
@@ -103,9 +102,8 @@
         pltpu.make_async_copy(resident_keys, kv.at[pl.ds(0, held), :, pl.ds(0, kw)], load_sem.at[0]),
         pltpu.make_async_copy(resident_vals, kv.at[pl.ds(0, held), :, pl.ds(kw, kw)], load_sem.at[1]),
         pltpu.make_async_copy(w_query, wcat.at[:, pl.ds(0, qw)], load_sem.at[2]),
-        pltpu.make_async_copy(w_key, wcat.at[:, pl.ds(qw, kw)], load_sem.at[3]),
-        pltpu.make_async_copy(w_val, wcat.at[:, pl.ds(qw + kw, kw)], load_sem.at[4]),
-        pltpu.make_async_copy(w_out, wout, load_sem.at[5]),
+        pltpu.make_async_copy(w_keyval, wcat.at[:, pl.ds(qw, 2 * kw)], load_sem.at[3]),
+        pltpu.make_async_copy(w_out, wout, load_sem.at[4]),
     ]
     for load in loads:
         load.start()
@@ -268,7 +266,7 @@
 
         @pl.when(k == 0)
         def _():
-            for load in loads[2:5]:
+            for load in loads[2:4]:
                 load.wait()
 
         def project(c, carry):
@@ -332,16 +330,23 @@
         column = lax.broadcasted_iota(jnp.int32, (group * BLOCK, total), 1)
         token = lax.rem(lax.broadcasted_iota(jnp.int32, (group * BLOCK, total), 0), BLOCK)
         seen = (column < length) | ((column >= context) & (column - context <= k * BLOCK + token))
-        for g in range(n_kv):
-            at = g * HD
-            scores = lax.dot_general(
+        scale = math.log2(math.e) / math.sqrt(HD)
+
+        def score(g):
+            return lax.dot_general(
                 heads[g * group * BLOCK : (g + 1) * group * BLOCK, :],
-                kv[:, :, at : at + HD].reshape(total, HD),
+                kv[:, :, g * HD : (g + 1) * HD].reshape(total, HD),
                 (((1,), (1,)), ((), ())),
                 preferred_element_type=jnp.float32,
             )
-            scores = jnp.where(seen, scores * (1.0 / math.sqrt(HD)), -1e30)
-            powers = jnp.exp(scores - jnp.max(scores, axis=-1, keepdims=True))
+
+        upcoming = score(0)
+        for g in range(n_kv):
+            at = g * HD
+            scores = jnp.where(seen, upcoming, -1e30)
+            if g + 1 < n_kv:
+                upcoming = score(g + 1)
+            powers = jnp.exp2((scores - jnp.max(scores, axis=-1, keepdims=True)) * scale)
             total_power = jnp.sum(powers, axis=-1, keepdims=True)
             got = jnp.dot(
                 powers.astype(jnp.bfloat16),
@@ -357,7 +362,7 @@
 
         @pl.when(k == 0)
         def _():
-            loads[5].wait()
+            loads[4].wait()
 
         @pl.when(k == BLOCKS - 1)
         def _():
@@ -375,31 +380,34 @@
         @pl.when(k == 1)
         def _():
             ship_mixed(mixed_count * 4 // 9, mixed_count * 7 // 9)
+
+        active = layer_on[s].astype(jnp.float32)
+
+        def finish(c):
+            ex(c).wait()
+            own = mixed[pl.ds(pl.multiple_of(t * half, BLOCK), half), cols(c)].astype(jnp.float32)
+            summed = own + mixed_in[:, cols(c)].astype(jnp.float32)
+            base = own_x[k, :, cols(c)].astype(jnp.float32)
+            out[k, :, cols(c)] = (base + active * summed).astype(jnp.bfloat16)
+
+            @pl.when((k < BLOCKS - 1) & (s < S - 1))
+            def _():
+                hand(k, c).start()
 
         def project_out(c, carry):
             mixed[:, cols(c)] = jnp.dot(
                 attended[...], wout[:, cols(c)], preferred_element_type=jnp.float32
             ).astype(jnp.bfloat16)
             ex(c).start()
+
+            @pl.when(c > 0)
+            def _():
+                finish(c - 1)
+
             return carry
 
         lax.fori_loop(0, n_out, project_out, 0)
-        active = layer_on[s].astype(jnp.float32)
-
-        def finish(c, carry):
-            ex(c).wait()
-            own = mixed[pl.ds(pl.multiple_of(t * half, BLOCK), half), cols(c)].astype(jnp.float32)
-            summed = own + mixed_in[:, cols(c)].astype(jnp.float32)
-            base = own_x[k, :, cols(c)].astype(jnp.float32)
-            out[k, :, cols(c)] = (base + active * summed).astype(jnp.bfloat16)
-
-            @pl.when((k < BLOCKS - 1) & (s < S - 1))
-            def _():
-                hand(k, c).start()
-
-            return carry
-
-        lax.fori_loop(0, n_out, finish, 0)
+        finish(jnp.int32(n_out - 1))
         return carry
 
     lax.fori_loop(0, BLOCKS, step_body, 0)
@@ -523,7 +531,7 @@
             jax.ShapeDtypeStruct((dests, cap) + page_shape, bf16),
             jax.ShapeDtypeStruct((BLOCKS, R, S) + page_shape, bf16),
         ),
-        in_specs=[smem] * 3 + [vmem] * 6 + [anywhere] * 6,
+        in_specs=[smem] * 3 + [vmem] * 6 + [anywhere] * 5,
         out_specs=(vmem, anywhere, vmem if dests <= 16 else anywhere),
         scratch_shapes=[
             pltpu.VMEM((width_block, qw + 2 * kw), bf16),
@@ -541,7 +549,7 @@
             pltpu.VMEM((rows, qw), bf16),
             pltpu.VMEM((rows, out_width), bf16),
             pltpu.VMEM((token_rows, out_width), bf16),
-            dma((6,)),
+            dma((5,)),
             dma((n_out,)),
             dma((n_out,)),
             dma((R,)),
@@ -577,8 +585,7 @@
         keyval_bias[0],
         freq,
         w_query[0],
-        w_keyval[0, :, 0],
-        w_keyval[0, :, 1],
+        w_keyval[0].reshape(width_block, 2 * kw),
         w_out[0],
         resident[:, :, 0],
         resident[:, :, 1],

time: 197 us -> 192 us (0.975)
  local copies, waits for them, and re-layouts: 21.6 us -> 15.5 us
    slice x1 -> x0, local copies, waits for them, and re-layouts: 8.94 us -> none  [local(): w_keyval[0, :, 1]]
    unnamed x12 -> x9, local copies, waits for them, and re-layouts: 3.15 us -> 9.37 us
    squeeze x1 -> x0, local copies, waits for them, and re-layouts: 3.3 us -> none  [local(): w_keyval[0, :, 1]]
where the time goes in v1:
time: 192 us; the launch traced here: 190 us
  Pallas kernels  170 us (89%)
  local copies, waits for them, and re-layouts  15.5 us (8%)
  other arithmetic  3.21 us (2%)
    pallas_call x1, Pallas kernels, local(): pl.pallas_call(functools.partial(steps_kernel, (R, S, context)), out_shap...  167 us
    unnamed x9, local copies, waits for them, and re-layouts  9.37 us

profile of v1, /device:TPU:8, one launch (start us, length us, event | category | flops | bytes accessed | tf_op | source)
XLA Modules:
  0.0 189.5 jit_solution(9889091358776626474)
XLA Ops:
  0.6 0.7 broadcast_compare_fusion.1
  1.3 0.1 gt.12
  1.4 0.7 broadcast_add_fusion
  2.1 0.1 add.81
  2.2 0.8 slice_reduce_fusion
  3.1 0.1 eq.78
  3.2 0.1 eq.77
  3.3 0.1 copy.24
  3.4 0.1 copy.23
  3.5 0.8 convert_reduce_fusion
  4.3 0.2 add_reduce_fusion
  4.5 0.1 copy.26
  4.6 0.1 reshape.166
  4.7 0.1 select_reduce_fusion
  4.8 0.6 select_reduce_fusion.1.pack_pages
  5.4 2.0 %copy.25 = bf16[1,1,1120,2,512]{4,2,3,1,0:T(8,128)(2,1)S(1)} copy(bf16[1,1,1120,2,512]{4,3,2,1,0:T(2,128)(2,1)} %param.21) | data formatting | bytes 4587520 | tf_op args[8]
  7.5 0.0 copy-start.1
  7.5 1.5 slice_bitcast_fusion
  9.0 1.5 copy-done.1
  10.5 3.1 %copy.28 = bf16[256,8,2,512]{3,1,2,0:T(8,128)(2,1)} copy(bf16[256,8,2,512]{3,2,1,0:T(2,128)(2,1)S(1)} %bitcast.28) | data formatting | bytes 8388608
  13.6 166.9 %relay_steps.1 = (bf16[3,64,2048]{2,1,0:T(8,128)(2,1)}, bf16[16,3,32,1024]{3,2,1,0:T(8,128)(2,1)}, bf16[3,4,4,32,1024]{4,3,2,1,0:T(8,128)(2,1)}) custom-call(s32[4]{0:T(128)} %resumed.1, s32[4]{0:T(128)} %layer_on.1, s32[48]{0:T(128)} %select_reduce_fusion.1.pack_pages, bf16[64,2048]{1,0:T(8,128)(2,1)} %bitcast.31, bf16[2,64,2048]{2,1,0:T(8,128)(2,1)} %arriving.1, ...), custom_call_target="tpu_custom_call" | custom-call | tf_op jit(solution)/shard_map/relay_steps/pallas_call | solution.py:527
  180.5 0.0 copy-start
  180.5 1.9 copy-done
  182.4 3.2 %place_pages.1 = bf16[38,32,1024]{2,1,0:T(8,128)(2,1)S(1)} custom-call(s32[38]{0:T(128)S(1)} %get-tuple-element.13.kind, s32[38]{0:T(128)S(1)} %get-tuple-element.12.place, bf16[48,32,1024]{2,1,0:T(8,128)(2,1)S(1)} %bitcast.23, bf16[48,32,1024]{2,1,0:T(8,128)(2,1)} %bitcast.29), custom_call_target="tpu_custom_call" | custom-call | tf_op jit(solution)/shard_map/place_pages/pallas_call | solution.py:594
  185.6 0.0 copy-start.2
  185.6 3.0 %reshape.160 = bf16[1,1,38,32,2,512]{5,4,3,2,1,0:T(2,128)(2,1)} reshape(bf16[38,32,1024]{2,1,0:T(8,128)(2,1)S(1)} %place_pages.1) | data formatting | bytes 4980736 | tf_op jit(solution)/shard_map/reshape | solution.py:607
  188.6 0.0 copy-done.2
  188.6 0.9 copy.30
  (9 shorter events, 0.1 us)
Async XLA Ops:
  7.5 3.0 %copy-start.1 = (bf16[1,2048,2,512]{3,2,1,0:T(2,128)(2,1)S(1)}, bf16[1,2048,2,512]{3,2,1,0:T(2,128)(2,1)}, u32[]{:S(2)}) copy-start(bf16[1,2048,2,512]{3,2,1,0:T(2,128)(2,1)} %param.16) | copy-start | bytes 12582916
  180.5 1.9 copy-start
  185.6 3.1 %copy-start.2 = (bf16[3,64,2048]{2,1,0:T(8,128)(2,1)S(1)}, bf16[3,64,2048]{2,1,0:T(8,128)(2,1)}, u32[]{:S(2)}) copy-start(bf16[3,64,2048]{2,1,0:T(8,128)(2,1)} %get-tuple-element.5) | copy-start | bytes 2359300

commit v2 on v1

--- a/solution.py
+++ b/solution.py
@@ -279,9 +279,13 @@
 
         lax.fori_loop(0, n_rs, project, 0)
 
-        @pl.when(k > 0)
-        def _():
-            spread(k - 1)
+        @pl.when(k == 1)
+        def _():
+            ship_mixed(mixed_count * 2 // 9, mixed_count * 4 // 9)
+
+        @pl.when(k == 2)
+        def _():
+            ship_mixed(mixed_count * 7 // 9, mixed_count)
 
         for j in range(1, R):
             sq(j).wait()
@@ -366,20 +370,11 @@
 
         @pl.when(k == BLOCKS - 1)
         def _():
-            ship_mixed(mixed_count * 7 // 9, mixed_count)
             spread(BLOCKS - 1)
 
         for g in range(n_kv):
             for j in range(1, R):
                 ag(g, j).wait()
-
-        @pl.when(k == 0)
-        def _():
-            ship_mixed(0, mixed_count * 4 // 9)
-
-        @pl.when(k == 1)
-        def _():
-            ship_mixed(mixed_count * 4 // 9, mixed_count * 7 // 9)
 
         active = layer_on[s].astype(jnp.float32)
 
@@ -408,6 +403,19 @@
 
         lax.fori_loop(0, n_out, project_out, 0)
         finish(jnp.int32(n_out - 1))
+
+        @pl.when(k < BLOCKS - 1)
+        def _():
+            spread(k)
+
+        @pl.when(k == 0)
+        def _():
+            ship_mixed(0, mixed_count * 2 // 9)
+
+        @pl.when(k == 1)
+        def _():
+            ship_mixed(mixed_count * 4 // 9, mixed_count * 7 // 9)
+
         return carry
 
     lax.fori_loop(0, BLOCKS, step_body, 0)

time: 192 us -> 181 us (0.943)
  Pallas kernels: 170 us -> 161 us
    pallas_call x1, Pallas kernels: 167 us -> 158 us  [local(): pl.pallas_call(functools.partial(steps_kernel, (R, S, context)), out_shap...]
where the time goes in v2:
time: 181 us; the launch traced here: 180 us
  Pallas kernels  161 us (89%)
  local copies, waits for them, and re-layouts  15.5 us (9%)
  other arithmetic  3.21 us (2%)
    pallas_call x1, Pallas kernels, local(): pl.pallas_call(functools.partial(steps_kernel, (R, S, context)), out_shap...  158 us
    unnamed x9, local copies, waits for them, and re-layouts  9.37 us

profile of v2, /device:TPU:8, one launch (start us, length us, event | category | flops | bytes accessed | tf_op | source)
XLA Modules:
  0.0 180.2 jit_solution(8867790180349551136)
XLA Ops:
  0.6 0.7 broadcast_compare_fusion.1
  1.3 0.1 gt.12
  1.4 0.7 broadcast_add_fusion
  2.1 0.1 add.81
  2.2 0.8 slice_reduce_fusion
  3.1 0.1 eq.78
  3.2 0.1 eq.77
  3.3 0.1 copy.24
  3.4 0.1 copy.23
  3.5 0.8 convert_reduce_fusion
  4.3 0.2 add_reduce_fusion
  4.5 0.1 copy.26
  4.6 0.1 reshape.166
  4.7 0.1 select_reduce_fusion
  4.8 0.6 select_reduce_fusion.1.pack_pages
  5.4 2.0 %copy.25 = bf16[1,1,1120,2,512]{4,2,3,1,0:T(8,128)(2,1)S(1)} copy(bf16[1,1,1120,2,512]{4,3,2,1,0:T(2,128)(2,1)} %param.21) | data formatting | bytes 4587520 | tf_op args[8]
  7.5 0.0 copy-start.1
  7.5 1.5 slice_bitcast_fusion
  9.0 1.5 copy-done.1
  10.5 3.1 %copy.28 = bf16[256,8,2,512]{3,1,2,0:T(8,128)(2,1)} copy(bf16[256,8,2,512]{3,2,1,0:T(2,128)(2,1)S(1)} %bitcast.28) | data formatting | bytes 8388608
  13.6 157.6 %relay_steps.1 = (bf16[3,64,2048]{2,1,0:T(8,128)(2,1)}, bf16[16,3,32,1024]{3,2,1,0:T(8,128)(2,1)}, bf16[3,4,4,32,1024]{4,3,2,1,0:T(8,128)(2,1)}) custom-call(s32[4]{0:T(128)} %resumed.1, s32[4]{0:T(128)} %layer_on.1, s32[48]{0:T(128)} %select_reduce_fusion.1.pack_pages, bf16[64,2048]{1,0:T(8,128)(2,1)} %bitcast.31, bf16[2,64,2048]{2,1,0:T(8,128)(2,1)} %arriving.1, ...), custom_call_target="tpu_custom_call" | custom-call | tf_op jit(solution)/shard_map/relay_steps/pallas_call | solution.py:535
  171.2 0.0 copy-start
  171.2 1.9 %copy-done = bf16[16,3,32,1024]{3,2,1,0:T(8,128)(2,1)S(1)} copy-done((bf16[16,3,32,1024]{3,2,1,0:T(8,128)(2,1)S(1)}, bf16[16,3,32,1024]{3,2,1,0:T(8,128)(2,1)}, u32[]{:S(2)}) %copy-start) | copy-done | bytes 3145752
  173.1 3.2 %place_pages.1 = bf16[38,32,1024]{2,1,0:T(8,128)(2,1)S(1)} custom-call(s32[38]{0:T(128)S(1)} %get-tuple-element.13.kind, s32[38]{0:T(128)S(1)} %get-tuple-element.12.place, bf16[48,32,1024]{2,1,0:T(8,128)(2,1)S(1)} %bitcast.23, bf16[48,32,1024]{2,1,0:T(8,128)(2,1)} %bitcast.29), custom_call_target="tpu_custom_call" | custom-call | tf_op jit(solution)/shard_map/place_pages/pallas_call | solution.py:602
  176.2 0.0 copy-start.2
  176.3 3.0 %reshape.160 = bf16[1,1,38,32,2,512]{5,4,3,2,1,0:T(2,128)(2,1)} reshape(bf16[38,32,1024]{2,1,0:T(8,128)(2,1)S(1)} %place_pages.1) | data formatting | bytes 4980736 | tf_op jit(solution)/shard_map/reshape | solution.py:615
  179.3 0.0 copy-done.2
  179.3 0.9 copy.30
  (9 shorter events, 0.1 us)
Async XLA Ops:
  7.5 3.0 %copy-start.1 = (bf16[1,2048,2,512]{3,2,1,0:T(2,128)(2,1)S(1)}, bf16[1,2048,2,512]{3,2,1,0:T(2,128)(2,1)}, u32[]{:S(2)}) copy-start(bf16[1,2048,2,512]{3,2,1,0:T(2,128)(2,1)} %param.16) | copy-start | bytes 12582916
  171.2 1.9 %copy-start = (bf16[16,3,32,1024]{3,2,1,0:T(8,128)(2,1)S(1)}, bf16[16,3,32,1024]{3,2,1,0:T(8,128)(2,1)}, u32[]{:S(2)}) copy-start(bf16[16,3,32,1024]{3,2,1,0:T(8,128)(2,1)} %get-tuple-element.6) | copy-start | bytes 9437188
  176.2 3.1 %copy-start.2 = (bf16[3,64,2048]{2,1,0:T(8,128)(2,1)S(1)}, bf16[3,64,2048]{2,1,0:T(8,128)(2,1)}, u32[]{:S(2)}) copy-start(bf16[3,64,2048]{2,1,0:T(8,128)(2,1)} %get-tuple-element.5) | copy-start | bytes 2359300

commit v3 on v2

--- a/solution.py
+++ b/solution.py
@@ -283,10 +283,6 @@
         def _():
             ship_mixed(mixed_count * 2 // 9, mixed_count * 4 // 9)
 
-        @pl.when(k == 2)
-        def _():
-            ship_mixed(mixed_count * 7 // 9, mixed_count)
-
         for j in range(1, R):
             sq(j).wait()
         ms = [squares[rows_of(r), :]] + [squares_in[rows_of(behind(j)), :] for j in range(1, R)]
@@ -329,6 +325,10 @@
         own_page(k).start()
         for j in range(1, S):
             fz(k, j).start()
+
+        @pl.when(k == BLOCKS - 1)
+        def _():
+            ship_mixed(mixed_count * 7 // 9, mixed_count)
 
         total = kv.shape[0] * PAGE
         column = lax.broadcasted_iota(jnp.int32, (group * BLOCK, total), 1)

time: 181 us -> 185 us (1.022)
  Pallas kernels: 161 us -> 163 us
    pallas_call x1, Pallas kernels: 158 us -> 160 us  [local(): pl.pallas_call(functools.partial(steps_kernel, (R, S, context)), out_shap...]
where the time goes in v3:
time: 185 us; the launch traced here: 183 us
  Pallas kernels  163 us (88%)
  local copies, waits for them, and re-layouts  15.5 us (8%)
  other arithmetic  3.21 us (2%)
    pallas_call x1, Pallas kernels, local(): pl.pallas_call(functools.partial(steps_kernel, (R, S, context)), out_shap...  160 us
    unnamed x9, local copies, waits for them, and re-layouts  9.37 us

profile of v3, /device:TPU:8, one launch (start us, length us, event | category | flops | bytes accessed | tf_op | source)
XLA Modules:
  0.0 182.9 jit_solution(11167645152894625471)
XLA Ops:
  0.6 0.7 broadcast_compare_fusion.1
  1.3 0.1 gt.12
  1.4 0.7 broadcast_add_fusion
  2.1 0.1 add.81
  2.2 0.8 slice_reduce_fusion
  3.1 0.1 eq.78
  3.2 0.1 eq.77
  3.3 0.1 copy.24
  3.4 0.1 copy.23
  3.5 0.8 convert_reduce_fusion
  4.3 0.2 add_reduce_fusion
  4.5 0.1 copy.26
  4.6 0.1 reshape.166
  4.7 0.1 select_reduce_fusion
  4.8 0.6 select_reduce_fusion.1.pack_pages
  5.4 2.0 %copy.25 = bf16[1,1,1120,2,512]{4,2,3,1,0:T(8,128)(2,1)S(1)} copy(bf16[1,1,1120,2,512]{4,3,2,1,0:T(2,128)(2,1)} %param.21) | data formatting | bytes 4587520 | tf_op args[8]
  7.5 0.0 copy-start.1
  7.5 1.5 slice_bitcast_fusion
  9.0 1.5 copy-done.1
  10.5 3.1 %copy.28 = bf16[256,8,2,512]{3,1,2,0:T(8,128)(2,1)} copy(bf16[256,8,2,512]{3,2,1,0:T(2,128)(2,1)S(1)} %bitcast.28) | data formatting | bytes 8388608
  13.6 160.3 %relay_steps.1 = (bf16[3,64,2048]{2,1,0:T(8,128)(2,1)}, bf16[16,3,32,1024]{3,2,1,0:T(8,128)(2,1)}, bf16[3,4,4,32,1024]{4,3,2,1,0:T(8,128)(2,1)}) custom-call(s32[4]{0:T(128)} %resumed.1, s32[4]{0:T(128)} %layer_on.1, s32[48]{0:T(128)} %select_reduce_fusion.1.pack_pages, bf16[64,2048]{1,0:T(8,128)(2,1)} %bitcast.31, bf16[2,64,2048]{2,1,0:T(8,128)(2,1)} %arriving.1, ...), custom_call_target="tpu_custom_call" | custom-call | tf_op jit(solution)/shard_map/relay_steps/pallas_call | solution.py:535
  173.9 0.0 copy-start
  173.9 1.9 %copy-done = bf16[16,3,32,1024]{3,2,1,0:T(8,128)(2,1)S(1)} copy-done((bf16[16,3,32,1024]{3,2,1,0:T(8,128)(2,1)S(1)}, bf16[16,3,32,1024]{3,2,1,0:T(8,128)(2,1)}, u32[]{:S(2)}) %copy-start) | copy-done | bytes 3145752
  175.8 3.2 %place_pages.1 = bf16[38,32,1024]{2,1,0:T(8,128)(2,1)S(1)} custom-call(s32[38]{0:T(128)S(1)} %get-tuple-element.13.kind, s32[38]{0:T(128)S(1)} %get-tuple-element.12.place, bf16[48,32,1024]{2,1,0:T(8,128)(2,1)S(1)} %bitcast.23, bf16[48,32,1024]{2,1,0:T(8,128)(2,1)} %bitcast.29), custom_call_target="tpu_custom_call" | custom-call | tf_op jit(solution)/shard_map/place_pages/pallas_call | solution.py:602
  179.0 0.0 copy-start.2
  179.0 3.0 %reshape.160 = bf16[1,1,38,32,2,512]{5,4,3,2,1,0:T(2,128)(2,1)} reshape(bf16[38,32,1024]{2,1,0:T(8,128)(2,1)S(1)} %place_pages.1) | data formatting | bytes 4980736 | tf_op jit(solution)/shard_map/reshape | solution.py:615
  182.0 0.0 copy-done.2
  182.0 0.9 copy.30
  (9 shorter events, 0.1 us)
Async XLA Ops:
  7.5 3.0 %copy-start.1 = (bf16[1,2048,2,512]{3,2,1,0:T(2,128)(2,1)S(1)}, bf16[1,2048,2,512]{3,2,1,0:T(2,128)(2,1)}, u32[]{:S(2)}) copy-start(bf16[1,2048,2,512]{3,2,1,0:T(2,128)(2,1)} %param.16) | copy-start | bytes 12582916
  173.9 1.9 %copy-start = (bf16[16,3,32,1024]{3,2,1,0:T(8,128)(2,1)S(1)}, bf16[16,3,32,1024]{3,2,1,0:T(8,128)(2,1)}, u32[]{:S(2)}) copy-start(bf16[16,3,32,1024]{3,2,1,0:T(8,128)(2,1)} %get-tuple-element.6) | copy-start | bytes 9437188
  179.0 3.1 %copy-start.2 = (bf16[3,64,2048]{2,1,0:T(8,128)(2,1)S(1)}, bf16[3,64,2048]{2,1,0:T(8,128)(2,1)}, u32[]{:S(2)}) copy-start(bf16[3,64,2048]{2,1,0:T(8,128)(2,1)} %get-tuple-element.5) | copy-start | bytes 2359300
